TPU v7x, 512 devices: a whole 4x8x8 slice. The times are simulated.
512 devices in a mesh: mode: 8 (over y_hi, core), pen: 64 (over y_lo, z, x).
Axes of the slice: x: 4, y: 8 (y_hi: 4, y_lo: 2; y = y_hi * 2 + y_lo), z: 8, core: 2. Of those that a mesh axis runs over, the one named last changes fastest.
Arguments:
- object_field: bfloat16 [2, 256, 256, 256], P(None, 'pen'), may hold values from -6 to 6
- probes: bfloat16 [8, 2, 256, 256, 256], P('mode', None, 'pen'), may hold values from -3 to 3
- measured: float32 [256, 256, 256], P(None, 'pen'), may hold values from 8 to 128
Outputs:
- gradient: float32 [2, 256, 256, 256], P(None, 'pen', 'mode')
All inputs are finite; a program needn't handle non-finite values.
Results may differ from a plain program's by a relative error of at most 0.0003.
Values sent between devices are 32-bit elements; how exact they have to be, the bound alone decides.
A program may use at most 64 MiB of HBM per device.

v0:
```python
import functools
import math

import jax
import jax.numpy as jnp
import ml_dtypes
import numpy as np
from jax import lax
from jax.experimental import pallas as pl
from jax.experimental.pallas import tpu as pltpu
from jax.sharding import PartitionSpec as P

DAMP = 0.1
N = 256
H = N // 2
F32 = jnp.float32
BF16 = jnp.bfloat16
MESH = pl.DeviceIdType.MESH


def forward_matrix(parity):
    freq = 2 * np.arange(H) + parity
    angle = 2.0 * math.pi / N * ((freq[:, None] * np.arange(H)[None, :]) % N)
    cosine, sine = np.cos(angle) / math.sqrt(N), np.sin(angle) / math.sqrt(N)
    return np.block([[cosine, sine], [-sine, cosine]])


def inverse_matrix(parity):
    return forward_matrix(parity).T


def split(matrix):
    high = matrix.astype(ml_dtypes.bfloat16)
    low = (matrix - high.astype(np.float64)).astype(ml_dtypes.bfloat16)
    return np.stack([high, low])


def tables():
    slab, part, row = np.meshgrid(np.arange(H // 4), np.arange(2), np.arange(4), indexing="ij")
    order = (part * H + slab * 4 + row).reshape(-1)
    sets = []
    for parity in range(2):
        fwd, inv = forward_matrix(parity), inverse_matrix(parity)
        sets.append(
            [split(fwd.T), split(fwd), split(fwd[:, order]), split(inv[order, :]), split(inv), split(inv.T)]
        )
    weights = np.stack([np.stack([sets[0][k], sets[1][k]]) for k in range(6)])
    rows = np.zeros((N, N), np.float32)
    rows[np.arange(N), np.concatenate([np.arange(0, N, 2), np.arange(1, N, 2)])] = 1.0
    return weights, rows


def halves(value):
    high = value.astype(BF16)
    return high, (value - high.astype(F32)).astype(BF16)


def dot(left, right):
    return jnp.dot(left, right, preferred_element_type=F32)


def table_first(table, value):
    high, low = halves(value)
    return dot(table[0], high) + (dot(table[0], low) + dot(table[1], high))


def table_last(value, table):
    high, low = halves(value)
    return dot(high, table[0]) + (dot(low, table[0]) + dot(high, table[1]))


def place():
    mode, pen = lax.axis_index("mode"), lax.axis_index("pen")
    return dict(
        mode=mode, pen=pen, y_hi=mode // 2, core=mode % 2, y=(mode // 2) * 2 + pen // 32, z=(pen // 4) % 8, x=pen % 4
    )


def chip_at(me, step):
    t = (step * 181) % 256
    x, y, z = (me["x"] + t % 4) % 4, (me["y"] + (t // 4) % 8) % 8, (me["z"] + t // 32) % 8
    return y // 2, (y % 2) * 32 + z * 4 + x


def z_peer(me, step):
    return {"pen": me["pen"] // 32 * 32 + (me["z"] + step) % 8 * 4 + me["x"]}


def xy_peer(me, step):
    other = (me["pen"] // 32 * 4 + me["x"] + step) % 8
    return {"pen": other // 4 * 32 + me["z"] * 4 + other % 4}


def mode_peer(me, step):
    return {"mode": (me["mode"] + step) % 8}


def greet(semaphore, me, *kinds):
    for kind in kinds:
        for step in range(1, 8):
            pl.semaphore_signal(semaphore, inc=1, device_id=kind(me, step), device_id_type=MESH)


def meet_all(me, lines, planes):
    barrier = pltpu.get_barrier_semaphore()
    greet(barrier, me, mode_peer, z_peer, xy_peer)
    pl.semaphore_wait(barrier, 21)
    greet(lines, me, z_peer)
    pl.semaphore_wait(lines, 7)
    greet(planes, me, xy_peer)
    pl.semaphore_wait(planes, 7)


def ship(source, target, ssem, rsem, device):
    return pltpu.make_async_remote_copy(
        src_ref=source, dst_ref=target, send_sem=ssem, recv_sem=rsem, device_id=device, device_id_type=MESH
    )


def wait_bytes(ref, sem):
    pltpu.make_async_copy(ref, ref, sem).wait()


def exit_wave(obj, prb, x):
    p_re, p_im = prb[0, x].astype(F32), prb[1, x].astype(F32)
    o_re, o_im = obj[0, x].astype(F32), obj[1, x].astype(F32)
    return p_re, p_im, p_re * o_re - p_im * o_im, p_re * o_im + p_im * o_re


def transform_zy(obj, prb, meas, wz, wy, perm, send, root):
    me = place()
    own = meas[:, pl.ds(me["y_hi"], 1), :].reshape(N, N)
    rows = jnp.dot(perm[...], jnp.sqrt(own), precision=lax.Precision.HIGHEST, preferred_element_type=F32)
    root[...] = lax.dot_general(
        rows, perm[pl.ds(pl.multiple_of(me["core"] * H, H), H), :], (((1,), (1,)), ((), ())),
        precision=lax.Precision.HIGHEST, preferred_element_type=F32,
    )
    for half in range(2):
        for two in range(2):
            lines = []
            for x in (2 * two, 2 * two + 1):
                _, _, e_re, e_im = exit_wave(obj, prb, x)
                if half == 0:
                    mixed = jnp.concatenate([e_re[:, :H] + e_re[:, H:], e_im[:, :H] + e_im[:, H:]], axis=1)
                else:
                    mixed = jnp.concatenate([e_re[:, :H] - e_re[:, H:], e_im[:, :H] - e_im[:, H:]], axis=1)
                lines.append(table_last(mixed, wz[half]))
            re = jnp.concatenate([lines[0][:, :H], lines[1][:, :H]], axis=1)
            im = jnp.concatenate([lines[0][:, H:], lines[1][:, H:]], axis=1)
            for parity in range(2):
                if parity == 0:
                    mixed = jnp.concatenate([re[:H] + re[H:], im[:H] + im[H:]], axis=0)
                else:
                    mixed = jnp.concatenate([re[:H] - re[H:], im[:H] - im[H:]], axis=0)
                result = table_first(wy[parity], mixed)
                flat = send.at[pl.ds(half * N, N)].reshape(N * 8, H)
                for c in range(2):
                    for k in range(2):
                        rows = pl.ds(parity * 8 + c * 4 + 2 * two + k, H, stride=16)
                        flat[rows, :] = result[c * H : (c + 1) * H, k * H : (k + 1) * H]


def send_half(me, half, source, target, send_sem, recv_sem):
    @pl.loop(1, 256)
    def _(step):
        y_hi, pen = chip_at(me, step)
        mode = y_hi * 2 + half
        ship(source(mode, pen), target, send_sem, recv_sem, {"mode": mode, "pen": pen}).start()


def send_home(me, source, target, send_sem, recv_sem, own_sem):
    sibling = me["y_hi"] * 2 + 1 - me["core"]
    ship(source(sibling, me["pen"]), target, send_sem, recv_sem, {"mode": sibling}).start()
    own = pltpu.make_async_copy(source(me["mode"], me["pen"]), target, own_sem)
    own.start()
    own.wait()


def exchange(
    send, root, wx, vx, ret, recv, lines, planes, send_sem, recv_sem, back_sem, ret_sem, own_sem
):
    me = place()
    meet_all(me, lines, planes)

    def tile(mode, pen):
        return send.at[mode % 2 * N + 4 * pen + mode // 2]

    landing = recv.at[me["mode"] * 64 + me["pen"]]
    for half in range(2):
        send_half(me, half, tile, landing, send_sem, recv_sem)
    send_home(me, tile, landing, send_sem, recv_sem, own_sem)
    wait_bytes(recv.at[pl.ds(0, 511)], recv_sem)

    def slab(mode):
        return recv.at[pl.ds(64 * mode, 64)].reshape(2 * N, H)

    power = [jnp.zeros((H, H), F32), jnp.zeros((H, H), F32)]
    for two in range(4):
        value = jnp.concatenate([slab(2 * two + k)[...] for k in range(2)], axis=1)
        top, bottom = value[:N], value[N:]
        for parity in range(2):
            result = table_first(wx[parity], top + bottom if parity == 0 else top - bottom)
            for k in range(2):
                slab(2 * two + k)[parity * N : (parity + 1) * N, :] = result[:, k * H : (k + 1) * H]
            square = result * result
            square = square[:H] + square[H:]
            power[parity] = power[parity] + (square[:, :H] + square[:, H:])
    ratio = [root[parity * H : (parity + 1) * H] / jnp.sqrt(power[parity] + DAMP) for parity in range(2)]
    ratio = [jnp.concatenate([r, r], axis=0) for r in ratio]
    ratio = [jnp.concatenate([r, r], axis=1) for r in ratio]

    def home(mode, pen):
        return recv.at[mode * 64 + pen]

    target = ret.at[me["core"] * N + 4 * me["pen"] + me["y_hi"]]
    for half in range(2):
        for two in range(2):
            modes = (4 * two + half, 4 * two + 2 + half)
            parts = []
            for parity in range(2):
                rows = slice(parity * N, (parity + 1) * N)
                value = jnp.concatenate([slab(mode)[rows, :] for mode in modes], axis=1)
                parts.append(table_first(vx[parity], value * ratio[parity]))
            for side in range(2):
                result = parts[0] + parts[1] if side == 0 else parts[0] - parts[1]
                for k in range(2):
                    slab(modes[k])[side * N : (side + 1) * N, :] = result[:, k * H : (k + 1) * H]
        send_half(me, half, home, target, back_sem, ret_sem)
    send_home(me, home, target, back_sem, ret_sem, own_sem)
    wait_bytes(ret.at[pl.ds(0, 511)], ret_sem)
    wait_bytes(ret.at[pl.ds(0, 511)], back_sem)
    wait_bytes(ret.at[pl.ds(0, 511)], send_sem)


def update(
    obj, prb, ret, vy, vz, out, part, pair, total, early, near,
    pair_send, pair_recv, early_send, early_recv, near_send, near_recv,
):
    me = place()
    core, other, y_hi = me["core"], 1 - me["core"], me["y_hi"]
    barrier = pltpu.get_barrier_semaphore()
    greet(barrier, me, mode_peer)
    ways = (1, 3)

    def chip(d):
        return {"mode": (y_hi + d) % 4 * 2 + core}

    def to_core(x):
        return ship(
            part.at[other, x], pair.at[x], pair_send.at[x], pair_recv.at[x], {"mode": y_hi * 2 + other}
        )

    def early_to(x, way):
        return ship(
            total.at[x, (y_hi + 2) % 4, way], early.at[x, way], early_send.at[x, way], early_recv.at[x, way],
            chip(ways[way]),
        )

    def near_to(x, way):
        return ship(
            total.at[x, (y_hi + ways[way]) % 4], near.at[x, way], near_send.at[x, way], near_recv.at[x, way],
            chip(ways[way]),
        )

    def first(x):
        to_core(x).wait_recv()
        total[x] = part[core, x] + pair[x]
        for way in range(2):
            early_to(x, way).start()

    def second(x):
        for way in range(2):
            early_to(x, way).wait_recv()
            total[x, (y_hi + ways[way]) % 4, way] += early[x, way]
            near_to(x, way).start()

    for two in range(2):
        columns = []
        for half in range(2):
            flat = ret.at[pl.ds(half * N, N)].reshape(N * 8, H)
            pieces = []
            for parity in range(2):
                blocks = [
                    [flat[pl.ds(parity * 8 + c * 4 + 2 * two + k, H, stride=16), :] for k in range(2)]
                    for c in range(2)
                ]
                value = jnp.concatenate([jnp.concatenate(b, axis=1) for b in blocks], axis=0)
                pieces.append(table_first(vy[parity], value))
            columns.append((pieces[0] + pieces[1], pieces[0] - pieces[1]))
        for k in range(2):
            x = 2 * two + k
            lanes = slice(k * H, (k + 1) * H)
            lines = []
            for half in range(2):
                top, bottom = columns[half]
                re = jnp.concatenate([top[:H, lanes], bottom[:H, lanes]], axis=0)
                im = jnp.concatenate([top[H:, lanes], bottom[H:, lanes]], axis=0)
                lines.append(table_last(jnp.concatenate([re, im], axis=1), vz[half]))
            low, high = lines[0] + lines[1], lines[0] - lines[1]
            p_re, p_im, e_re, e_im = exit_wave(obj, prb, x)
            d_re = jnp.concatenate([low[:, :H], high[:, :H]], axis=1) - e_re
            d_im = jnp.concatenate([low[:, H:], high[:, H:]], axis=1) - e_im
            g_re = p_re * d_re + p_im * d_im
            g_im = p_re * d_im - p_im * d_re
            for chunk in range(8):
                rows = slice(32 * chunk, 32 * chunk + 32)
                part[chunk % 2, x, chunk // 2, 0] = g_re[rows]
                part[chunk % 2, x, chunk // 2, 1] = g_im[rows]
            if x == 0:
                pl.semaphore_wait(barrier, 7)
            to_core(x).start()
            if x > 0:
                first(x - 1)
            if x > 1:
                second(x - 2)
    first(3)
    second(2)
    second(3)
    for x in range(4):
        for way in range(2):
            near_to(x, way).wait_recv()
        out[:, x] = total[x, y_hi] + (near[x, 0] + near[x, 1])
    for x in range(4):
        to_core(x).wait_send()
        for way in range(2):
            early_to(x, way).wait_send()
            near_to(x, way).wait_send()


def call(body, name, number, inputs, results, scratch):
    fields = dict(collective_id=number, has_side_effects=True) if number is not None else {}
    vmem = pl.BlockSpec(memory_space=pltpu.VMEM)
    return pl.pallas_call(
        body,
        out_shape=[jax.ShapeDtypeStruct(shape, F32) for shape in results],
        in_specs=[vmem] * len(inputs),
        out_specs=[vmem] * len(results),
        scratch_shapes=scratch,
        compiler_params=pltpu.CompilerParams(vmem_limit_bytes=40 * 2**20, **fields),
        name=name,
    )(*inputs)


def shards(object_field, probes, measured):
    weights, rows = tables()
    wz, wy, wx, vx, vy, vz = [jnp.asarray(weights[k]) for k in range(6)]
    vmem, dma, regular = pltpu.VMEM, pltpu.SemaphoreType.DMA, pltpu.SemaphoreType.REGULAR
    prb = probes[0]
    tiles = (512, 8, H)
    send, root = call(
        transform_zy, "transform_zy", None, (object_field, prb, measured, wz, wy, jnp.asarray(rows)),
        (tiles, (N, H)), [],
    )
    (ret,) = call(
        exchange, "exchange", 0, (send, root, wx, vx), (tiles,),
        [vmem(tiles, F32), regular, regular, dma, dma, dma, dma, dma],
    )
    (gradient,) = call(
        update, "update", 1, (object_field, prb, ret, vy, vz), ((2, 4, 32, N),),
        [
            vmem((2, 4, 4, 2, 32, N), F32),
            vmem((4, 4, 2, 32, N), F32),
            vmem((4, 4, 2, 32, N), F32),
            vmem((4, 2, 32, N), F32),
            vmem((4, 2, 2, 32, N), F32),
            dma((4,)), dma((4,)), dma((4, 2)), dma((4, 2)), dma((4, 2)), dma((4, 2)),
        ],
    )
    return gradient


def solution(mesh):
    return jax.shard_map(
        shards,
        mesh=mesh,
        in_specs=(
            P(None, "pen", None, None),
            P("mode", None, "pen", None, None),
            P(None, "pen", None),
        ),
        out_specs=P(None, "pen", "mode", None),
        check_vma=False,
    )
```

profile of v0, /device:TPU:6, one launch (start us, length us, event | category | flops | bytes accessed | tf_op | source)
XLA Modules:
  0.0 152.6 jit_solution(5343140151085710725)
XLA Ops:
  0.0 0.0 copy-start
  0.0 1.2 copy-done
  1.2 0.0 copy-start.2
  1.2 1.2 copy-done.2
  2.5 0.0 copy-start.4
  2.5 1.0 copy-done.4
  3.5 0.0 copy-start.6
  3.5 1.0 copy-done.6
  4.5 0.0 copy-start.8
  4.5 1.2 copy-done.8
  5.8 0.0 copy-start.11
  5.8 0.9 copy-done.11
  6.7 0.0 copy-start.9
  6.7 0.0 copy-start.10
  6.7 4.3 %transform_zy.1 = (f32[512,8,128]{2,1,0:T(8,128)S(1)}, f32[256,128]{1,0:T(8,128)S(1)}) custom-call(bf16[2,4,256,256]{3,2,1,0:T(8,128)(2,1)S(1)} %copy-done, bf16[2,4,256,256]{3,2,1,0:T(8,128)(2,1)S(1)} %bitcast.1, f32[256,4,256]{2,1,0:T(4,128)S(1)} %copy-done.8, bf16[2,2,256,256]{3,2,1,0:T(8,128)(2,1)S(1)} %copy-done.6, ...), custom_call_target="tpu_custom_call" | custom-call | tf_op jit(solution)/shard_map/transform_zy/pallas_call | solution.py:333
  11.0 0.0 copy-done.9
  11.0 0.0 copy-done.10
  11.0 0.0 copy-start.1
  11.0 0.0 copy-start.3
  11.1 0.0 copy-start.5
  11.1 0.0 copy-start.7
  11.1 100.1 %exchange.1.ret = f32[512,8,128]{2,1,0:T(8,128)S(1)} custom-call(f32[512,8,128]{2,1,0:T(8,128)S(1)} %get-tuple-element.7.send, f32[256,128]{1,0:T(8,128)S(1)} %get-tuple-element.8.root, bf16[2,2,256,256]{3,2,1,0:T(8,128)(2,1)S(1)} %copy-done.10, bf16[2,2,256,256]{3,2,1,0:T(8,128)(2,1)S(1)} %copy-done.9), custom_call_target="tpu_custom_call" | custom-call | tf_op jit(solution)/shard_map/exchange/pallas_call | solution.py:333
  111.2 0.0 copy-done.1
  111.2 0.0 copy-done.3
  111.2 0.0 copy-done.5
  111.3 0.0 copy-done.7
  111.3 40.7 %update.1 = f32[2,4,32,256]{3,2,1,0:T(8,128)S(1)} custom-call(bf16[2,4,256,256]{3,2,1,0:T(8,128)(2,1)S(1)} %copy-done.1, bf16[2,4,256,256]{3,2,1,0:T(8,128)(2,1)S(1)} %bitcast.2, f32[512,8,128]{2,1,0:T(8,128)S(1)} %exchange.1.ret, bf16[2,2,256,256]{3,2,1,0:T(8,128)(2,1)S(1)} %copy-done.7, bf16[2,2,256,256]{3,2,1,0:T(8,128)(2,1)S(1)} %copy-done.5), custom_call_target="tpu_custom_call" | custom-call | tf_op jit(solution)/shard_map/update/pallas_call | solution.py:333
  151.9 0.7 copy.12
Async XLA Ops:
  0.0 1.2 copy-start
  1.2 1.2 copy-start.2
  2.5 1.0 copy-start.4
  3.5 1.0 copy-start.6
  4.5 1.2 copy-start.8
  5.8 0.9 copy-start.11
  6.7 4.3 %copy-start.9 = (bf16[2,2,256,256]{3,2,1,0:T(8,128)(2,1)S(1)}, bf16[2,2,256,256]{3,2,1,0:T(8,128)(2,1)}, u32[]{:S(2)}) copy-start(bf16[2,2,256,256]{3,2,1,0:T(8,128)(2,1)} %constant.13.clone.vx) | copy-start | bytes 1572868
  6.7 4.3 %copy-start.10 = (bf16[2,2,256,256]{3,2,1,0:T(8,128)(2,1)S(1)}, bf16[2,2,256,256]{3,2,1,0:T(8,128)(2,1)}, u32[]{:S(2)}) copy-start(bf16[2,2,256,256]{3,2,1,0:T(8,128)(2,1)} %constant.12.clone.wx) | copy-start | bytes 1572868
  11.0 100.2 %copy-start.1 = (bf16[2,4,256,256]{3,2,1,0:T(8,128)(2,1)S(1)}, bf16[2,4,256,256]{3,2,1,0:T(8,128)(2,1)}, u32[]{:S(2)}) copy-start(bf16[2,4,256,256]{3,2,1,0:T(8,128)(2,1)} %obj.3) | copy-start | bytes 3145732
  11.0 100.2 %copy-start.3 = (bf16[1,2,4,256,256]{4,3,2,1,0:T(8,128)(2,1)S(1)}, bf16[1,2,4,256,256]{4,3,2,1,0:T(8,128)(2,1)}, u32[]{:S(2)}) copy-start(bf16[1,2,4,256,256]{4,3,2,1,0:T(8,128)(2,1)} %param.11) | copy-start | bytes 3145732
  11.1 100.2 %copy-start.5 = (bf16[2,2,256,256]{3,2,1,0:T(8,128)(2,1)S(1)}, bf16[2,2,256,256]{3,2,1,0:T(8,128)(2,1)}, u32[]{:S(2)}) copy-start(bf16[2,2,256,256]{3,2,1,0:T(8,128)(2,1)} %constant.11.clone.wy.vz) | copy-start | bytes 1572868
  11.1 100.2 %copy-start.7 = (bf16[2,2,256,256]{3,2,1,0:T(8,128)(2,1)S(1)}, bf16[2,2,256,256]{3,2,1,0:T(8,128)(2,1)}, u32[]{:S(2)}) copy-start(bf16[2,2,256,256]{3,2,1,0:T(8,128)(2,1)} %constant.10.clone.wz.vy) | copy-start | bytes 1572868
where the time goes:
time: 153 us
  Pallas kernels  145 us (95%)
  local copies, waits for them, and re-layouts  7.44 us (5%)
    pallas_call x3, Pallas kernels, call(): pl.pallas_call(body, out_shape=[jax.ShapeDtypeStruct(shape, F32) for shap...  145 us
    unnamed x25, local copies, waits for them, and re-layouts  7.44 us

commit v1 on v0

--- a/solution.py
+++ b/solution.py
@@ -44,10 +44,7 @@
         sets.append(
             [split(fwd.T), split(fwd), split(fwd[:, order]), split(inv[order, :]), split(inv), split(inv.T)]
         )
-    weights = np.stack([np.stack([sets[0][k], sets[1][k]]) for k in range(6)])
-    rows = np.zeros((N, N), np.float32)
-    rows[np.arange(N), np.concatenate([np.arange(0, N, 2), np.arange(1, N, 2)])] = 1.0
-    return weights, rows
+    return np.stack([np.stack([sets[0][k], sets[1][k]]) for k in range(6)])
 
 
 def halves(value):
@@ -127,23 +124,58 @@
     return p_re, p_im, p_re * o_re - p_im * o_im, p_re * o_im + p_im * o_re
 
 
-def transform_zy(obj, prb, meas, wz, wy, perm, send, root):
+def magnitudes(me, own):
+    own = jnp.sqrt(own)
+    row, column = (lax.broadcasted_iota(jnp.int32, (N, N), k) for k in range(2))
+    evens_first = (column == row % H * 2 + row // H).astype(F32)
+    rows = jnp.dot(evens_first, own, precision=lax.Precision.HIGHEST, preferred_element_type=F32)
+    row, column = (lax.broadcasted_iota(jnp.int32, (N, H), k) for k in range(2))
+    chosen = (row == column * 2 + me["core"]).astype(F32)
+    return jnp.dot(rows, chosen, precision=lax.Precision.HIGHEST, preferred_element_type=F32)
+
+
+def transform_zy(
+    obj_in, prb_in, meas_in, wz_in, wy_in, send, own, obj, prb, meas, wz, wy, obj_sem, prb_sem, sem
+):
     me = place()
-    own = meas[:, pl.ds(me["y_hi"], 1), :].reshape(N, N)
-    rows = jnp.dot(perm[...], jnp.sqrt(own), precision=lax.Precision.HIGHEST, preferred_element_type=F32)
-    root[...] = lax.dot_general(
-        rows, perm[pl.ds(pl.multiple_of(me["core"] * H, H), H), :], (((1,), (1,)), ((), ())),
-        precision=lax.Precision.HIGHEST, preferred_element_type=F32,
-    )
+
+    def obj_row(x):
+        return pltpu.make_async_copy(obj_in.at[:, x], obj.at[:, x], obj_sem.at[x])
+
+    def prb_row(x):
+        return pltpu.make_async_copy(prb_in.at[:, x], prb.at[:, x], prb_sem.at[x])
+
+    table_z = pltpu.make_async_copy(wz_in, wz, sem.at[0])
+    table_y = pltpu.make_async_copy(wy_in, wy, sem.at[1])
+    intensities = [
+        pltpu.make_async_copy(meas_in.at[pl.ds(64 * k, 64)], meas.at[pl.ds(64 * k, 64)], sem.at[2 + k]) for k in range(4)
+    ]
+    for x in range(2):
+        obj_row(x).start()
+        prb_row(x).start()
+    table_z.start()
+    table_y.start()
+    for x in range(2, 4):
+        obj_row(x).start()
+        prb_row(x).start()
+    for k in range(4):
+        intensities[k].start()
+
     for half in range(2):
         for two in range(2):
             lines = []
             for x in (2 * two, 2 * two + 1):
+                if half == 0:
+                    obj_row(x).wait()
+                    prb_row(x).wait()
                 _, _, e_re, e_im = exit_wave(obj, prb, x)
                 if half == 0:
                     mixed = jnp.concatenate([e_re[:, :H] + e_re[:, H:], e_im[:, :H] + e_im[:, H:]], axis=1)
                 else:
                     mixed = jnp.concatenate([e_re[:, :H] - e_re[:, H:], e_im[:, :H] - e_im[:, H:]], axis=1)
+                if half == 0 and x == 0:
+                    table_z.wait()
+                    table_y.wait()
                 lines.append(table_last(mixed, wz[half]))
             re = jnp.concatenate([lines[0][:, :H], lines[1][:, :H]], axis=1)
             im = jnp.concatenate([lines[0][:, H:], lines[1][:, H:]], axis=1)
@@ -158,6 +190,9 @@
                     for k in range(2):
                         rows = pl.ds(parity * 8 + c * 4 + 2 * two + k, H, stride=16)
                         flat[rows, :] = result[c * H : (c + 1) * H, k * H : (k + 1) * H]
+    for k in range(4):
+        intensities[k].wait()
+    own[...] = meas[:, pl.ds(me["y_hi"], 1), :].reshape(N, N)
 
 
 def send_half(me, half, source, target, send_sem, recv_sem):
@@ -177,7 +212,7 @@
 
 
 def exchange(
-    send, root, wx, vx, ret, recv, lines, planes, send_sem, recv_sem, back_sem, ret_sem, own_sem
+    send, own, wx, vx, ret, recv, lines, planes, send_sem, recv_sem, back_sem, ret_sem, own_sem
 ):
     me = place()
     meet_all(me, lines, planes)
@@ -189,6 +224,7 @@
     for half in range(2):
         send_half(me, half, tile, landing, send_sem, recv_sem)
     send_home(me, tile, landing, send_sem, recv_sem, own_sem)
+    root = magnitudes(me, own[...])
     wait_bytes(recv.at[pl.ds(0, 511)], recv_sem)
 
     def slab(mode):
@@ -327,32 +363,38 @@
             near_to(x, way).wait_send()
 
 
-def call(body, name, number, inputs, results, scratch):
+def call(body, name, number, inputs, results, scratch, limit=40, space=pltpu.VMEM):
     fields = dict(collective_id=number, has_side_effects=True) if number is not None else {}
-    vmem = pl.BlockSpec(memory_space=pltpu.VMEM)
     return pl.pallas_call(
         body,
         out_shape=[jax.ShapeDtypeStruct(shape, F32) for shape in results],
-        in_specs=[vmem] * len(inputs),
-        out_specs=[vmem] * len(results),
+        in_specs=[pl.BlockSpec(memory_space=space)] * len(inputs),
+        out_specs=[pl.BlockSpec(memory_space=pltpu.VMEM)] * len(results),
         scratch_shapes=scratch,
-        compiler_params=pltpu.CompilerParams(vmem_limit_bytes=40 * 2**20, **fields),
+        compiler_params=pltpu.CompilerParams(vmem_limit_bytes=limit * 2**20, **fields),
         name=name,
     )(*inputs)
 
 
 def shards(object_field, probes, measured):
-    weights, rows = tables()
+    weights = tables()
     wz, wy, wx, vx, vy, vz = [jnp.asarray(weights[k]) for k in range(6)]
     vmem, dma, regular = pltpu.VMEM, pltpu.SemaphoreType.DMA, pltpu.SemaphoreType.REGULAR
     prb = probes[0]
     tiles = (512, 8, H)
-    send, root = call(
-        transform_zy, "transform_zy", None, (object_field, prb, measured, wz, wy, jnp.asarray(rows)),
-        (tiles, (N, H)), [],
+    slab = (2, 4, N, N)
+    send, own = call(
+        transform_zy, "transform_zy", None, tuple(
+            pltpu.with_memory_space_constraint(a, pltpu.HBM) for a in (object_field, prb, measured, wz, wy)
+        ), (tiles, (N, N)),
+        [
+            vmem(slab, BF16), vmem(slab, BF16), vmem((N, 4, N), F32), vmem(wz.shape, BF16), vmem(wy.shape, BF16),
+            dma((4,)), dma((4,)), dma((6,)),
+        ],
+        space=pl.ANY,
     )
     (ret,) = call(
-        exchange, "exchange", 0, (send, root, wx, vx), (tiles,),
+        exchange, "exchange", 0, (send, own, wx, vx), (tiles,),
         [vmem(tiles, F32), regular, regular, dma, dma, dma, dma, dma],
     )
     (gradient,) = call(

time: 153 us -> 148 us (0.967)
  local copies, waits for them, and re-layouts: 7.44 us -> 0.74 us
  Pallas kernels: 145 us -> 147 us
    unnamed x25 -> x13, local copies, waits for them, and re-layouts: 7.44 us -> 0.74 us
    pallas_call x3, Pallas kernels: 145 us -> 147 us  [call(): pl.pallas_call(body, out_shape=[jax.ShapeDtypeStruct(shape, F32) for shap...]
where the time goes in v1:
time: 148 us
  Pallas kernels  147 us (99%)
    pallas_call x3, Pallas kernels, call(): pl.pallas_call(body, out_shape=[jax.ShapeDtypeStruct(shape, F32) for shap...  147 us

profile of v1, /device:TPU:6, one launch (start us, length us, event | category | flops | bytes accessed | tf_op | source)
XLA Modules:
  0.0 148.0 jit_solution(2244462005030957080)
XLA Ops:
  0.0 0.0 copy-start.4
  0.0 0.0 copy-start.5
  0.0 5.7 %transform_zy.1 = (f32[512,8,128]{2,1,0:T(8,128)S(1)}, f32[256,256]{1,0:T(8,128)S(1)}) custom-call(bf16[2,4,256,256]{3,2,1,0:T(8,128)(2,1)} %obj.1, bf16[2,4,256,256]{3,2,1,0:T(8,128)(2,1)} %bitcast.1, f32[256,4,256]{2,1,0:T(4,128)} %meas_in.1, bf16[2,2,256,256]{3,2,1,0:T(8,128)(2,1)} %constant.8.clone.wz_in.vy, bf16[2,2,256,256]{3,2,1,0:T(8,128)(2,1)} %constant.9.clone.wy_in.vz), custom_call_target="tpu_custom_call" | custom-call | tf_op jit(solution)/shard_map/transform_zy/pallas_call | solution.py:368
  5.7 0.0 copy-done.4
  5.7 0.0 copy-done.5
  5.7 0.0 copy-start
  5.7 0.0 copy-start.1
  5.7 0.0 copy-start.2
  5.8 0.0 copy-start.3
  5.8 100.1 %exchange.1.ret = f32[512,8,128]{2,1,0:T(8,128)S(1)} custom-call(f32[512,8,128]{2,1,0:T(8,128)S(1)} %get-tuple-element.7.send, f32[256,256]{1,0:T(8,128)S(1)} %get-tuple-element.8.own, bf16[2,2,256,256]{3,2,1,0:T(8,128)(2,1)S(1)} %copy-done.5, bf16[2,2,256,256]{3,2,1,0:T(8,128)(2,1)S(1)} %copy-done.4), custom_call_target="tpu_custom_call" | custom-call | tf_op jit(solution)/shard_map/exchange/pallas_call | solution.py:368
  105.9 0.0 copy-done
  105.9 0.0 copy-done.1
  105.9 0.0 copy-done.2
  105.9 0.0 copy-done.3
  105.9 41.4 %update.1 = f32[2,4,32,256]{3,2,1,0:T(8,128)S(1)} custom-call(bf16[2,4,256,256]{3,2,1,0:T(8,128)(2,1)S(1)} %copy-done, bf16[2,4,256,256]{3,2,1,0:T(8,128)(2,1)S(1)} %bitcast.2, f32[512,8,128]{2,1,0:T(8,128)S(1)} %exchange.1.ret, bf16[2,2,256,256]{3,2,1,0:T(8,128)(2,1)S(1)} %copy-done.3, bf16[2,2,256,256]{3,2,1,0:T(8,128)(2,1)S(1)} %copy-done.2), custom_call_target="tpu_custom_call" | custom-call | tf_op jit(solution)/shard_map/update/pallas_call | solution.py:368
  147.3 0.7 copy.11
Async XLA Ops:
  0.0 5.7 %copy-start.4 = (bf16[2,2,256,256]{3,2,1,0:T(8,128)(2,1)S(1)}, bf16[2,2,256,256]{3,2,1,0:T(8,128)(2,1)}, u32[]{:S(2)}) copy-start(bf16[2,2,256,256]{3,2,1,0:T(8,128)(2,1)} %constant.11.clone.vx) | copy-start | bytes 1572868
  0.0 5.7 %copy-start.5 = (bf16[2,2,256,256]{3,2,1,0:T(8,128)(2,1)S(1)}, bf16[2,2,256,256]{3,2,1,0:T(8,128)(2,1)}, u32[]{:S(2)}) copy-start(bf16[2,2,256,256]{3,2,1,0:T(8,128)(2,1)} %constant.10.clone.wx) | copy-start | bytes 1572868
  5.7 100.1 %copy-start = (bf16[2,4,256,256]{3,2,1,0:T(8,128)(2,1)S(1)}, bf16[2,4,256,256]{3,2,1,0:T(8,128)(2,1)}, u32[]{:S(2)}) copy-start(bf16[2,4,256,256]{3,2,1,0:T(8,128)(2,1)} %obj.1) | copy-start | bytes 3145732
  5.7 100.1 %copy-start.1 = (bf16[1,2,4,256,256]{4,3,2,1,0:T(8,128)(2,1)S(1)}, bf16[1,2,4,256,256]{4,3,2,1,0:T(8,128)(2,1)}, u32[]{:S(2)}) copy-start(bf16[1,2,4,256,256]{4,3,2,1,0:T(8,128)(2,1)} %param.10) | copy-start | bytes 3145732
  5.7 100.1 %copy-start.2 = (bf16[2,2,256,256]{3,2,1,0:T(8,128)(2,1)S(1)}, bf16[2,2,256,256]{3,2,1,0:T(8,128)(2,1)}, u32[]{:S(2)}) copy-start(bf16[2,2,256,256]{3,2,1,0:T(8,128)(2,1)} %constant.9.clone.wy_in.vz) | copy-start | bytes 1572868
  5.8 100.1 %copy-start.3 = (bf16[2,2,256,256]{3,2,1,0:T(8,128)(2,1)S(1)}, bf16[2,2,256,256]{3,2,1,0:T(8,128)(2,1)}, u32[]{:S(2)}) copy-start(bf16[2,2,256,256]{3,2,1,0:T(8,128)(2,1)} %constant.8.clone.wz_in.vy) | copy-start | bytes 1572868

commit v2 on v1

--- a/solution.py
+++ b/solution.py
@@ -96,16 +96,6 @@
     for kind in kinds:
         for step in range(1, 8):
             pl.semaphore_signal(semaphore, inc=1, device_id=kind(me, step), device_id_type=MESH)
-
-
-def meet_all(me, lines, planes):
-    barrier = pltpu.get_barrier_semaphore()
-    greet(barrier, me, mode_peer, z_peer, xy_peer)
-    pl.semaphore_wait(barrier, 21)
-    greet(lines, me, z_peer)
-    pl.semaphore_wait(lines, 7)
-    greet(planes, me, xy_peer)
-    pl.semaphore_wait(planes, 7)
 
 
 def ship(source, target, ssem, rsem, device):
@@ -215,15 +205,47 @@
     send, own, wx, vx, ret, recv, lines, planes, send_sem, recv_sem, back_sem, ret_sem, own_sem
 ):
     me = place()
-    meet_all(me, lines, planes)
+    barrier = pltpu.get_barrier_semaphore()
 
     def tile(mode, pen):
         return send.at[mode % 2 * N + 4 * pen + mode // 2]
 
     landing = recv.at[me["mode"] * 64 + me["pen"]]
-    for half in range(2):
-        send_half(me, half, tile, landing, send_sem, recv_sem)
-    send_home(me, tile, landing, send_sem, recv_sem, own_sem)
+
+    def pass_on(half, by_chip, by_xy):
+        mode = (me["y_hi"] + by_chip % 4) % 4 * 2 + half
+        z, xy = (me["z"] + by_chip // 4) % 8, (me["pen"] // 32 * 4 + me["x"] + by_xy) % 8
+        pen = xy // 4 * 32 + z * 4 + xy % 4
+
+        @pl.when((mode != me["mode"]) | (pen != me["pen"]))
+        def _():
+            ship(tile(mode, pen), landing, send_sem, recv_sem, {"mode": mode, "pen": pen}).start()
+
+    greet(barrier, me, mode_peer, z_peer, xy_peer)
+    pl.semaphore_wait(barrier, 21)
+    greet(lines, me, z_peer)
+    pl.semaphore_wait(lines, 7)
+    greet(planes, me, xy_peer)
+
+    @pl.loop(0, 32)
+    def _(step):
+        pass_on(0, step * 13 % 32, 0)
+
+    pl.semaphore_wait(planes, 7)
+
+    @pl.loop(0, 224)
+    def _(step):
+        t = step * 93 % 224
+        pass_on(0, t % 32, 1 + t // 32)
+
+    @pl.loop(0, 256)
+    def _(step):
+        t = step * 181 % 256
+        pass_on(1, t % 32, t // 32)
+
+    own_tile = pltpu.make_async_copy(tile(me["mode"], me["pen"]), landing, own_sem)
+    own_tile.start()
+    own_tile.wait()
     root = magnitudes(me, own[...])
     wait_bytes(recv.at[pl.ds(0, 511)], recv_sem)
 
@@ -275,11 +297,13 @@
     me = place()
     core, other, y_hi = me["core"], 1 - me["core"], me["y_hi"]
     barrier = pltpu.get_barrier_semaphore()
-    greet(barrier, me, mode_peer)
     ways = (1, 3)
 
     def chip(d):
         return {"mode": (y_hi + d) % 4 * 2 + core}
+
+    for device in ({"mode": y_hi * 2 + other}, chip(1), chip(3)):
+        pl.semaphore_signal(barrier, inc=1, device_id=device, device_id_type=MESH)
 
     def to_core(x):
         return ship(
@@ -343,7 +367,7 @@
                 part[chunk % 2, x, chunk // 2, 0] = g_re[rows]
                 part[chunk % 2, x, chunk // 2, 1] = g_im[rows]
             if x == 0:
-                pl.semaphore_wait(barrier, 7)
+                pl.semaphore_wait(barrier, 3)
             to_core(x).start()
             if x > 0:
                 first(x - 1)

time: 148 us -> 144 us (0.973)
  Pallas kernels: 147 us -> 143 us
    pallas_call x3, Pallas kernels: 147 us -> 143 us  [call(): pl.pallas_call(body, out_shape=[jax.ShapeDtypeStruct(shape, F32) for shap...]
where the time goes in v2:
time: 144 us
  Pallas kernels  143 us (99%)
    pallas_call x3, Pallas kernels, call(): pl.pallas_call(body, out_shape=[jax.ShapeDtypeStruct(shape, F32) for shap...  143 us

profile of v2, /device:TPU:6, one launch (start us, length us, event | category | flops | bytes accessed | tf_op | source)
XLA Modules:
  0.0 144.1 jit_solution(2332553147374482935)
XLA Ops:
  0.0 0.0 copy-start.4
  0.0 0.0 copy-start.5
  0.0 5.7 %transform_zy.1 = (f32[512,8,128]{2,1,0:T(8,128)S(1)}, f32[256,256]{1,0:T(8,128)S(1)}) custom-call(bf16[2,4,256,256]{3,2,1,0:T(8,128)(2,1)} %obj.1, bf16[2,4,256,256]{3,2,1,0:T(8,128)(2,1)} %bitcast.1, f32[256,4,256]{2,1,0:T(4,128)} %meas_in.1, bf16[2,2,256,256]{3,2,1,0:T(8,128)(2,1)} %constant.8.clone.wz_in.vy, bf16[2,2,256,256]{3,2,1,0:T(8,128)(2,1)} %constant.9.clone.wy_in.vz), custom_call_target="tpu_custom_call" | custom-call | tf_op jit(solution)/shard_map/transform_zy/pallas_call | solution.py:392
  5.7 0.0 copy-done.4
  5.7 0.0 copy-done.5
  5.7 0.0 copy-start
  5.7 0.0 copy-start.1
  5.7 0.0 copy-start.2
  5.8 0.0 copy-start.3
  5.8 98.2 %exchange.1.ret = f32[512,8,128]{2,1,0:T(8,128)S(1)} custom-call(f32[512,8,128]{2,1,0:T(8,128)S(1)} %get-tuple-element.7.send, f32[256,256]{1,0:T(8,128)S(1)} %get-tuple-element.8.own, bf16[2,2,256,256]{3,2,1,0:T(8,128)(2,1)S(1)} %copy-done.5, bf16[2,2,256,256]{3,2,1,0:T(8,128)(2,1)S(1)} %copy-done.4), custom_call_target="tpu_custom_call" | custom-call | tf_op jit(solution)/shard_map/exchange/pallas_call | solution.py:392
  103.9 0.0 copy-done
  103.9 0.0 copy-done.1
  104.0 0.0 copy-done.2
  104.0 0.0 copy-done.3
  104.0 39.5 %update.1 = f32[2,4,32,256]{3,2,1,0:T(8,128)S(1)} custom-call(bf16[2,4,256,256]{3,2,1,0:T(8,128)(2,1)S(1)} %copy-done, bf16[2,4,256,256]{3,2,1,0:T(8,128)(2,1)S(1)} %bitcast.2, f32[512,8,128]{2,1,0:T(8,128)S(1)} %exchange.1.ret, bf16[2,2,256,256]{3,2,1,0:T(8,128)(2,1)S(1)} %copy-done.3, bf16[2,2,256,256]{3,2,1,0:T(8,128)(2,1)S(1)} %copy-done.2), custom_call_target="tpu_custom_call" | custom-call | tf_op jit(solution)/shard_map/update/pallas_call | solution.py:392
  143.4 0.7 copy.11
Async XLA Ops:
  0.0 5.7 %copy-start.4 = (bf16[2,2,256,256]{3,2,1,0:T(8,128)(2,1)S(1)}, bf16[2,2,256,256]{3,2,1,0:T(8,128)(2,1)}, u32[]{:S(2)}) copy-start(bf16[2,2,256,256]{3,2,1,0:T(8,128)(2,1)} %constant.11.clone.vx) | copy-start | bytes 1572868
  0.0 5.7 %copy-start.5 = (bf16[2,2,256,256]{3,2,1,0:T(8,128)(2,1)S(1)}, bf16[2,2,256,256]{3,2,1,0:T(8,128)(2,1)}, u32[]{:S(2)}) copy-start(bf16[2,2,256,256]{3,2,1,0:T(8,128)(2,1)} %constant.10.clone.wx) | copy-start | bytes 1572868
  5.7 98.2 %copy-start = (bf16[2,4,256,256]{3,2,1,0:T(8,128)(2,1)S(1)}, bf16[2,4,256,256]{3,2,1,0:T(8,128)(2,1)}, u32[]{:S(2)}) copy-start(bf16[2,4,256,256]{3,2,1,0:T(8,128)(2,1)} %obj.1) | copy-start | bytes 3145732
  5.7 98.2 %copy-start.1 = (bf16[1,2,4,256,256]{4,3,2,1,0:T(8,128)(2,1)S(1)}, bf16[1,2,4,256,256]{4,3,2,1,0:T(8,128)(2,1)}, u32[]{:S(2)}) copy-start(bf16[1,2,4,256,256]{4,3,2,1,0:T(8,128)(2,1)} %param.10) | copy-start | bytes 3145732
  5.7 98.2 %copy-start.2 = (bf16[2,2,256,256]{3,2,1,0:T(8,128)(2,1)S(1)}, bf16[2,2,256,256]{3,2,1,0:T(8,128)(2,1)}, u32[]{:S(2)}) copy-start(bf16[2,2,256,256]{3,2,1,0:T(8,128)(2,1)} %constant.9.clone.wy_in.vz) | copy-start | bytes 1572868
  5.8 98.2 %copy-start.3 = (bf16[2,2,256,256]{3,2,1,0:T(8,128)(2,1)S(1)}, bf16[2,2,256,256]{3,2,1,0:T(8,128)(2,1)}, u32[]{:S(2)}) copy-start(bf16[2,2,256,256]{3,2,1,0:T(8,128)(2,1)} %constant.8.clone.wz_in.vy) | copy-start | bytes 1572868

commit v3 on v2

--- a/solution.py
+++ b/solution.py
@@ -212,36 +212,49 @@
 
     landing = recv.at[me["mode"] * 64 + me["pen"]]
 
-    def pass_on(half, by_chip, by_xy):
+    def pass_on(half, by_chip, by_xy, least):
         mode = (me["y_hi"] + by_chip % 4) % 4 * 2 + half
         z, xy = (me["z"] + by_chip // 4) % 8, (me["pen"] // 32 * 4 + me["x"] + by_xy) % 8
         pen = xy // 4 * 32 + z * 4 + xy % 4
-
-        @pl.when((mode != me["mode"]) | (pen != me["pen"]))
+        differ = [jnp.where(d, 1, 0) for d in (mode != me["mode"], by_chip // 4 != 0, by_xy != 0)]
+
+        @pl.when(differ[0] + differ[1] + differ[2] >= least)
         def _():
             ship(tile(mode, pen), landing, send_sem, recv_sem, {"mode": mode, "pen": pen}).start()
 
     greet(barrier, me, mode_peer, z_peer, xy_peer)
     pl.semaphore_wait(barrier, 21)
     greet(lines, me, z_peer)
+
+    @pl.loop(0, 4)
+    def _(step):
+        pass_on(0, step, 0, 1)
+
+    @pl.when(me["core"] == 0)
+    def _():
+        @pl.loop(1, 8)
+        def _(step):
+            pass_on(0, step * 4, 0, 1)
+            pass_on(0, 0, step, 1)
+
     pl.semaphore_wait(lines, 7)
     greet(planes, me, xy_peer)
 
     @pl.loop(0, 32)
     def _(step):
-        pass_on(0, step * 13 % 32, 0)
+        pass_on(0, step * 13 % 32, 0, 2)
 
     pl.semaphore_wait(planes, 7)
 
     @pl.loop(0, 224)
     def _(step):
         t = step * 93 % 224
-        pass_on(0, t % 32, 1 + t // 32)
+        pass_on(0, t % 32, 1 + t // 32, 2)
 
     @pl.loop(0, 256)
     def _(step):
         t = step * 181 % 256
-        pass_on(1, t % 32, t // 32)
+        pass_on(1, t % 32, t // 32, 1)
 
     own_tile = pltpu.make_async_copy(tile(me["mode"], me["pen"]), landing, own_sem)
     own_tile.start()

time: 144 us -> 145 us (level)
  the two profiles are of different devices: /device:TPU:6 before, /device:TPU:16 now
where the time goes in v3:
time: 145 us
  Pallas kernels  144 us (99%)
    pallas_call x3, Pallas kernels, call(): pl.pallas_call(body, out_shape=[jax.ShapeDtypeStruct(shape, F32) for shap...  144 us

profile of v3, /device:TPU:16, one launch (start us, length us, event | category | flops | bytes accessed | tf_op | source)
XLA Modules:
  0.0 145.0 jit_solution(3100972659750693565)
XLA Ops:
  0.0 0.0 copy-start.4
  0.0 0.0 copy-start.5
  0.0 5.7 %transform_zy.1 = (f32[512,8,128]{2,1,0:T(8,128)S(1)}, f32[256,256]{1,0:T(8,128)S(1)}) custom-call(bf16[2,4,256,256]{3,2,1,0:T(8,128)(2,1)} %obj.1, bf16[2,4,256,256]{3,2,1,0:T(8,128)(2,1)} %bitcast.1, f32[256,4,256]{2,1,0:T(4,128)} %meas_in.1, bf16[2,2,256,256]{3,2,1,0:T(8,128)(2,1)} %constant.8.clone.wz_in.vy, bf16[2,2,256,256]{3,2,1,0:T(8,128)(2,1)} %constant.9.clone.wy_in.vz), custom_call_target="tpu_custom_call" | custom-call | tf_op jit(solution)/shard_map/transform_zy/pallas_call | solution.py:405
  5.7 0.0 copy-done.4
  5.7 0.0 copy-done.5
  5.7 0.0 copy-start
  5.7 0.0 copy-start.1
  5.8 0.0 copy-start.2
  5.8 0.0 copy-start.3
  5.8 98.2 %exchange.1.ret = f32[512,8,128]{2,1,0:T(8,128)S(1)} custom-call(f32[512,8,128]{2,1,0:T(8,128)S(1)} %get-tuple-element.7.send, f32[256,256]{1,0:T(8,128)S(1)} %get-tuple-element.8.own, bf16[2,2,256,256]{3,2,1,0:T(8,128)(2,1)S(1)} %copy-done.5, bf16[2,2,256,256]{3,2,1,0:T(8,128)(2,1)S(1)} %copy-done.4), custom_call_target="tpu_custom_call" | custom-call | tf_op jit(solution)/shard_map/exchange/pallas_call | solution.py:405
  104.0 0.0 copy-done
  104.0 0.0 copy-done.1
  104.0 0.0 copy-done.2
  104.0 0.0 copy-done.3
  104.0 40.2 %update.1 = f32[2,4,32,256]{3,2,1,0:T(8,128)S(1)} custom-call(bf16[2,4,256,256]{3,2,1,0:T(8,128)(2,1)S(1)} %copy-done, bf16[2,4,256,256]{3,2,1,0:T(8,128)(2,1)S(1)} %bitcast.2, f32[512,8,128]{2,1,0:T(8,128)S(1)} %exchange.1.ret, bf16[2,2,256,256]{3,2,1,0:T(8,128)(2,1)S(1)} %copy-done.3, bf16[2,2,256,256]{3,2,1,0:T(8,128)(2,1)S(1)} %copy-done.2), custom_call_target="tpu_custom_call" | custom-call | tf_op jit(solution)/shard_map/update/pallas_call | solution.py:405
  144.2 0.7 copy.11
Async XLA Ops:
  0.0 5.7 %copy-start.4 = (bf16[2,2,256,256]{3,2,1,0:T(8,128)(2,1)S(1)}, bf16[2,2,256,256]{3,2,1,0:T(8,128)(2,1)}, u32[]{:S(2)}) copy-start(bf16[2,2,256,256]{3,2,1,0:T(8,128)(2,1)} %constant.11.clone.vx) | copy-start | bytes 1572868
  0.0 5.7 %copy-start.5 = (bf16[2,2,256,256]{3,2,1,0:T(8,128)(2,1)S(1)}, bf16[2,2,256,256]{3,2,1,0:T(8,128)(2,1)}, u32[]{:S(2)}) copy-start(bf16[2,2,256,256]{3,2,1,0:T(8,128)(2,1)} %constant.10.clone.wx) | copy-start | bytes 1572868
  5.7 98.3 %copy-start = (bf16[2,4,256,256]{3,2,1,0:T(8,128)(2,1)S(1)}, bf16[2,4,256,256]{3,2,1,0:T(8,128)(2,1)}, u32[]{:S(2)}) copy-start(bf16[2,4,256,256]{3,2,1,0:T(8,128)(2,1)} %obj.1) | copy-start | bytes 3145732
  5.7 98.3 %copy-start.1 = (bf16[1,2,4,256,256]{4,3,2,1,0:T(8,128)(2,1)S(1)}, bf16[1,2,4,256,256]{4,3,2,1,0:T(8,128)(2,1)}, u32[]{:S(2)}) copy-start(bf16[1,2,4,256,256]{4,3,2,1,0:T(8,128)(2,1)} %param.10) | copy-start | bytes 3145732
  5.8 98.3 %copy-start.2 = (bf16[2,2,256,256]{3,2,1,0:T(8,128)(2,1)S(1)}, bf16[2,2,256,256]{3,2,1,0:T(8,128)(2,1)}, u32[]{:S(2)}) copy-start(bf16[2,2,256,256]{3,2,1,0:T(8,128)(2,1)} %constant.9.clone.wy_in.vz) | copy-start | bytes 1572868
  5.8 98.3 %copy-start.3 = (bf16[2,2,256,256]{3,2,1,0:T(8,128)(2,1)S(1)}, bf16[2,2,256,256]{3,2,1,0:T(8,128)(2,1)}, u32[]{:S(2)}) copy-start(bf16[2,2,256,256]{3,2,1,0:T(8,128)(2,1)} %constant.8.clone.wz_in.vy) | copy-start | bytes 1572868
